TPU v7x, 32 devices: a whole 2x2x4 slice. The times are simulated.
32 devices in a mesh: rows: 32 (over z, y, x, core).
Axes of the slice: x: 2, y: 2, z: 4, core: 2. Of those that a mesh axis runs over, the one named last changes fastest.
Arguments:
- features: float32 [16384, 256], P('rows'), may hold values from -6 to 6
- adjacency: float32 [64, 6, 256, 256], P('rows'), may hold values from -0.25 to 0.25
- block_index: int32 [64, 6], P('rows'), may hold values from 0 to 63, as said below
- block_counts: int32 [64], P('rows'), may hold values from 1 to 6, as said below
- labels: int32 [16384], P('rows'), may hold values from 0 to 127
- weight_in: float32 [256, 512], replicated, may hold values from -0.375 to 0.375
- weight_out: float32 [512, 128], replicated, may hold values from -0.25 to 0.25
Outputs:
- logits: float32 [16384, 128], P('rows')
- mean_loss: float32 [], replicated
- hidden_grad: float32 [16384, 512], P('rows')
- grad_in: float32 [256, 512], replicated
- grad_out: float32 [512, 128], replicated
Inputs may be any that keep to these rules, and one draw needn't show every extreme that they name: `block_index`: row block b lies on device b // 2; every slot's column block lies at most 2 row blocks away from b, inside the graph. `block_counts`: some row block uses all 6 slots.
All inputs are finite; a program needn't handle non-finite values.
Results may differ from a plain program's by a relative error of at most 0.00011.
Values sent between devices are 32-bit elements; how exact they have to be, the bound alone decides.
A program may use at most 64 MiB of HBM per device.

v0:
```python
import jax
import jax.numpy as jnp
from jax import lax
from jax.sharding import PartitionSpec as P

REACH = 2


HIGH = lax.Precision.HIGHEST


def extended(block, sides, width):
    for axis, dim in sides:
        count = lax.axis_size(axis)
        forward = [(i, i + 1) for i in range(count - 1)]
        backward = [(target, source) for source, target in forward]
        low = lax.ppermute(
            lax.slice_in_dim(block, block.shape[dim] - width, None, axis=dim), axis, forward
        )
        high = lax.ppermute(lax.slice_in_dim(block, 0, width, axis=dim), axis, backward)
        block = jnp.concatenate([low, block, high], axis=dim)
    return block


def shifted(value, axis, steps):
    count = lax.axis_size(axis)
    first, last = (max(0, -steps), min(count, count - steps))
    return lax.ppermute(value, axis, [(source, source + steps) for source in range(first, last)])


def activate(values):
    return jax.nn.gelu(values, approximate=False)


def propagate(values, masked, relative):
    blocks_here = masked.shape[0]
    block_rows = masked.shape[2]
    width = values.shape[1]
    grouped = values.reshape(blocks_here, block_rows, width)
    nearby = extended(grouped, (("rows", 0),), REACH)
    picked = nearby[relative]
    result = jnp.einsum("bkij,bkjw->biw", masked, picked, precision=HIGH)
    return result.reshape(-1, width)


def transposed(grads, masked, relative):
    blocks_here, slot_total, block_rows = (masked.shape[0], masked.shape[1], masked.shape[2])
    width = grads.shape[1]
    terms = jnp.einsum(
        "bkij,biw->bkjw", masked, grads.reshape(blocks_here, block_rows, width), precision=HIGH
    )
    buckets_total = blocks_here + 2 * REACH
    selector = (
        relative.reshape(-1)[:, None] == jnp.arange(buckets_total, dtype=jnp.int32)[None, :]
    ).astype(jnp.float32)
    buckets = jnp.einsum(
        "ns,njw->sjw",
        selector,
        terms.reshape(blocks_here * slot_total, block_rows, width),
        precision=HIGH,
    )
    gathered = buckets[REACH : REACH + blocks_here]
    for heading in (1, -1):
        if heading == 1:
            outgoing = buckets[REACH + blocks_here :]
        else:
            outgoing = buckets[:REACH]
        arrived = shifted(outgoing, "rows", heading)
        if heading == 1:
            padded = arrived
        else:
            padded = arrived
        gathered = gathered + padded
    return gathered.reshape(-1, width)


def per_device(features, adjacency, block_index, block_counts, labels, weight_in, weight_out):
    blocks_here = adjacency.shape[0]
    slot_total = adjacency.shape[1]
    device_pos = lax.axis_index("rows")
    relative = block_index - (device_pos * blocks_here - REACH)
    usable = jnp.arange(slot_total, dtype=jnp.int32)[None, :] < block_counts[:, None]
    masked = jnp.where(usable[:, :, None, None], adjacency, jnp.zeros_like(adjacency))
    spread_in = propagate(features, masked, relative)
    pre_hidden = jnp.dot(spread_in, weight_in, precision=HIGH)
    hidden = activate(pre_hidden)
    spread_hidden = propagate(hidden, masked, relative)
    logits = jnp.dot(spread_hidden, weight_out, precision=HIGH)
    totals = jnp.log(jnp.sum(jnp.exp(logits), axis=1))
    onehot = (labels[:, None] == jnp.arange(logits.shape[1], dtype=jnp.int32)[None, :]).astype(
        jnp.float32
    )
    row_loss = totals - jnp.sum(onehot * logits, axis=1)
    loss_part = jnp.sum(row_loss)
    logit_grad = jnp.exp(logits - totals[:, None]) - onehot
    returned = transposed(logit_grad, masked, relative)
    grad_out = jnp.dot(spread_hidden.T, logit_grad, precision=HIGH)
    hidden_grad = jnp.dot(returned, weight_out.T, precision=HIGH)
    _, back = jax.vjp(activate, pre_hidden)
    pre_grad = back(hidden_grad)[0]
    grad_in = jnp.dot(spread_in.T, pre_grad, precision=HIGH)
    loss_total, grad_in, grad_out = lax.psum((loss_part, grad_in, grad_out), "rows")
    mean_loss = loss_total / (features.shape[0] * lax.axis_size("rows"))
    return (logits, mean_loss, hidden_grad, grad_in, grad_out)


def solution(mesh):
    in_specs = (
        P("rows", None),
        P("rows", None, None, None),
        P("rows", None),
        P("rows"),
        P("rows"),
        P(),
        P(),
    )
    out_specs = (P("rows", None), P(), P("rows", None), P(), P())
    return jax.shard_map(
        per_device, mesh=mesh, in_specs=in_specs, out_specs=out_specs, check_vma=False
    )
```

profile of v0, /device:TPU:0, one launch (start us, length us, event | category | flops | bytes accessed | tf_op | source)
XLA Modules:
  0.0 254.1 jit_solution(10510333916508259199)
XLA Ops:
  7.2 0.0 copy-start
  7.2 0.0 all-reduce.3.cloned.1.call-start
  7.2 1.4 collective-permute-start.1
  8.7 3.1 %collective-permute-start = (f32[2,256,256]{2,1,0:T(8,128)}, f32[2,256,256]{2,1,0:T(8,128)S(1)}, u32[]{:S(2)}, u32[]{:S(2)}) collective-permute-start(f32[2,256,256]{2,1,0:T(8,128)} %bitcast.47), channel_id=1, source_target_pairs={{0,1},{1,2},{2,3},{3,4},{4,5},{5,6},{6,7},{7,8},{8,9},{9,10},{10,1... | collective-permute-start | bytes 1572872 | tf_op jit(solution)/shard_map/ppermute | solution.py:17
  11.7 0.7 compare_select_fusion
  12.4 0.1 reshape.66
  12.5 0.7 iota_compare_fusion.2
  13.2 0.0 collective-permute-done.1
  13.2 0.2 collective-permute-done
  13.4 1.2 pad_maximum_fusion.1
  14.6 2.4 gather_fusion
  17.0 6.0 %fusion.4 = f32[2,256,256,1]{2,1,3,0:T(8,128)S(1)} fusion(f32[2,6,256,256]{3,2,1,0:T(8,128)} %bitcast.35, f32[2,6,256,256]{3,2,1,0:T(8,128)} %param.8, pred[2,6]{1,0:T(4,128)(4,1)S(1)} %iota_compare_fusion.2), kind=kOutput, calls=%fused_computation.7 | convolution fusion | flops 2416705536 | bytes 6815756 | tf_op jit(solution)/shard_map/bkij,bkjw->biw/dot_general | solution.py:42
  23.0 0.0 copy-done
  23.0 6.7 %multiply_multiply_fusion.5 = (f32[512,512]{1,0:T(8,128)S(1)}, f32[512,512]{1,0:T(8,128)}, f32[512,512]{1,0:T(8,128)}) fusion(f32[512,256]{1,0:T(8,128)S(1)} %bitcast.44, f32[256,512]{1,0:T(8,128)S(1)} %copy-done), kind=kOutput, calls=%fused_computation.44 | convolution fusion | flops 822083584 | bytes 4194304 | tf_op jit(solution)/shard_map/dot_general | solution.py:85
  29.7 1.3 collective-permute-start.3
  31.0 16.3 %collective-permute-start.2 = (f32[2,256,512]{2,1,0:T(8,128)S(1)}, f32[2,256,512]{2,1,0:T(8,128)}, u32[]{:S(2)}, u32[]{:S(2)}) collective-permute-start(f32[2,256,512]{2,1,0:T(8,128)S(1)} %bitcast.42), channel_id=1, source_target_pairs={{0,1},{1,2},{2,3},{3,4},{4,5},{5,6},{6,7},{7,8},{8,9},{9,10},{10,1... | collective-permute-start | bytes 3145736 | tf_op jit(solution)/shard_map/ppermute | solution.py:17
  47.3 0.1 eq.31
  47.4 0.0 collective-permute-done.3
  47.4 1.4 collective-permute-done.2
  48.8 3.3 %pad_maximum_fusion = f32[6,256,512]{2,1,0:T(8,128)} fusion(f32[2,256,512]{2,1,0:T(8,128)S(1)} %collective-permute-done.3, f32[2,256,512]{2,1,0:T(8,128)S(1)} %bitcast.43, f32[2,256,512]{2,1,0:T(8,128)} %collective-permute-done.2), kind=kLoop, calls=%fused_computation.2 | loop fusion | flops 1572864 | bytes 6291456 | tf_op jit(solution)/shard_map/concatenate | solution.py:21
  52.1 5.5 %gather_fusion.1 = f32[12,256,512]{2,1,0:T(8,128)} fusion(f32[6,256,512]{2,1,0:T(8,128)} %pad_maximum_fusion, s32[1024]{0:T(1024)S(1)} %pad_clamp_fusion), kind=kCustom, calls=%fused_computation.1 | custom fusion | bytes 12582960 | tf_op jit(solution)/shard_map/gather | solution.py:41
  57.6 9.6 %fusion.2 = f32[2,256,512,1]{2,1,3,0:T(8,128)S(1)} fusion(f32[2,6,256,512]{3,2,1,0:T(8,128)} %bitcast.34, f32[2,6,256,256]{3,2,1,0:T(8,128)} %param.8, pred[2,6]{1,0:T(4,128)(4,1)S(1)} %iota_compare_fusion.2), kind=kOutput, calls=%fused_computation.5 | convolution fusion | flops 4832624640 | bytes 10485772 | tf_op jit(solution)/shard_map/bkij,bkjw->biw/dot_general | solution.py:42
  67.2 0.0 copy-done.4
  67.2 0.0 copy-done.5
  67.2 1.1 exponential_reduce_fusion
  68.3 0.0 copy-start.3
  68.4 0.6 fusion.46
  69.0 0.2 convert_subtract_fusion
  69.2 0.0 copy-done.1
  69.2 5.2 %fusion = f32[2,6,256,128]{3,2,1,0:T(8,128)S(1)} fusion(f32[2,256,128,1]{2,1,3,0:T(8,128)S(1)} %bitcast.39, f32[2,6,256,256]{3,2,1,0:T(8,128)S(1)} %copy-done.1, pred[2,6]{1,0:T(4,128)(4,1)S(1)} %iota_compare_fusion.2), kind=kOutput, calls=%fused_computation.3 | convolution fusion | flops 1208745984 | bytes 4980748 | tf_op jit(solution)/shard_map/bkij,biw->bkjw/dot_general | solution.py:49
  74.4 1.7 fusion.6
  76.1 0.0 copy-done.3
  76.1 0.2 fusion.45
  76.3 22.0 %collective-permute-start.4 = (f32[2,256,128]{2,0,1:T(2,128)S(1)}, f32[2,256,128]{2,0,1:T(2,128)S(1)}, u32[]{:S(2)}, u32[]{:S(2)}) collective-permute-start(f32[2,256,128]{2,0,1:T(2,128)S(1)} %get-tuple-element.13), channel_id=1, source_target_pairs={{0,1},{1,2},{2,3},{3,4},{4,5},{5,6},{6,7},{7,8},{8,9},{9,10},{10,1... | collective-permute-start | bytes 786440 | tf_op jit(solution)/shard_map/ppermute | solution.py:28
  98.3 1.5 collective-permute-start.5
  99.9 2.5 fusion.48
  102.4 0.0 collective-permute-done.4
  102.4 0.7 collective-permute-done.5
  103.1 0.2 fusion.34
  103.4 1.0 fusion.47
  104.4 0.0 copy-start.2
  104.4 2.2 fusion.15
  106.7 0.0 all-reduce.3.cloned.1.call-update
  106.7 46.7 %psum.21 = f32[]{:T(128)} all-reduce(f32[]{:T(128)} %get-tuple-element.16), channel_id=1, replica_groups=mesh['rows'=32] {'rows'}, use_global_device_ids=true, to_apply=%region_3.4 | all-reduce | flops 1 | bytes 8 | tf_op jit(solution)/shard_map/psum | solution.py:102
  154.0 88.5 %all-reduce.3.cloned.1.call-done = (f32[256,512]{1,0:T(8,128)}, f32[512,128]{1,0:T(8,128)}) async-done(((f32[256,512]{1,0:T(8,128)}, f32[512,128]{1,0:T(8,128)}), (f32[256,512]{1,0:T(8,128)}, f32[512,128]{1,0:T(8,128)})) %all-reduce.3.cloned.1.call-update) | async-done | bytes 786448 | tf_op jit(solution)/shard_map/psum | solution.py:102
  242.5 1.9 copy.25
  244.4 0.0 copy-done.2
  244.4 1.7 copy.26
  (9 shorter events, 0.0 us)
Async XLA Ops:
  7.2 15.8 %copy-start = (f32[256,512]{1,0:T(8,128)S(1)}, f32[256,512]{1,0:T(8,128)}, u32[]{:S(2)}) copy-start(f32[256,512]{1,0:T(8,128)} %param.12) | copy-start | bytes 1572868
  7.2 235.4 %all-reduce.3.cloned.1.call-start = ((), (), s32[]{:S(2)}) async-start(), calls=%async_computation | async-start | bytes 1572864 | tf_op jit(solution)/shard_map/psum | solution.py:102
  7.2 6.0 %collective-permute-start.1 = (f32[2,256,256]{2,1,0:T(8,128)}, f32[2,256,256]{2,1,0:T(8,128)S(1)}, u32[]{:S(2)}, u32[]{:S(2)}) collective-permute-start(f32[2,256,256]{2,1,0:T(8,128)} %bitcast.46), channel_id=1, source_target_pairs={{1,0},{2,1},{3,2},{4,3},{5,4},{6,5},{7,6},{8,7},{9,8},{10,9},{11,1... | collective-permute-start | bytes 1572872 | tf_op jit(solution)/shard_map/ppermute | solution.py:20
  8.7 4.8 %collective-permute-start = (f32[2,256,256]{2,1,0:T(8,128)}, f32[2,256,256]{2,1,0:T(8,128)S(1)}, u32[]{:S(2)}, u32[]{:S(2)}) collective-permute-start(f32[2,256,256]{2,1,0:T(8,128)} %bitcast.47), channel_id=1, source_target_pairs={{0,1},{1,2},{2,3},{3,4},{4,5},{5,6},{6,7},{7,8},{8,9},{9,10},{10,1... | collective-permute-start | bytes 1572872 | tf_op jit(solution)/shard_map/ppermute | solution.py:17
  29.7 17.7 %collective-permute-start.3 = (f32[2,256,512]{2,1,0:T(8,128)S(1)}, f32[2,256,512]{2,1,0:T(8,128)S(1)}, u32[]{:S(2)}, u32[]{:S(2)}) collective-permute-start(f32[2,256,512]{2,1,0:T(8,128)S(1)} %bitcast.41), channel_id=1, source_target_pairs={{1,0},{2,1},{3,2},{4,3},{5,4},{6,5},{7,6},{8,7},{9,8},{10,9},{11,1... | collective-permute-start | bytes 3145736 | tf_op jit(solution)/shard_map/ppermute | solution.py:20
  31.0 17.7 %collective-permute-start.2 = (f32[2,256,512]{2,1,0:T(8,128)S(1)}, f32[2,256,512]{2,1,0:T(8,128)}, u32[]{:S(2)}, u32[]{:S(2)}) collective-permute-start(f32[2,256,512]{2,1,0:T(8,128)S(1)} %bitcast.42), channel_id=1, source_target_pairs={{0,1},{1,2},{2,3},{3,4},{4,5},{5,6},{6,7},{7,8},{8,9},{9,10},{10,1... | collective-permute-start | bytes 3145736 | tf_op jit(solution)/shard_map/ppermute | solution.py:17
  57.6 9.6 %copy-start.4 = (f32[512,128]{1,0:T(8,128)S(1)}, f32[512,128]{1,0:T(8,128)}, u32[]{:S(2)}) copy-start(f32[512,128]{1,0:T(8,128)} %param.13) | copy-start | bytes 786436
  57.6 9.6 %copy-start.5 = (s32[512]{0:T(512)S(1)}, s32[512]{0:T(512)}, u32[]{:S(2)}) copy-start(s32[512]{0:T(512)} %param.11) | copy-start | bytes 6148
  57.6 11.6 %copy-start.1 = (f32[2,6,256,256]{3,2,1,0:T(8,128)S(1)}, f32[2,6,256,256]{3,2,1,0:T(8,128)}, u32[]{:S(2)}) copy-start(f32[2,6,256,256]{3,2,1,0:T(8,128)} %param.8) | copy-start | bytes 9437188
  68.3 7.7 %copy-start.3 = (f32[512,128]{1,0:T(8,128)}, f32[512,128]{1,0:T(8,128)S(1)}, u32[]{:S(2)}) copy-start(f32[512,128]{1,0:T(8,128)S(1)} %get-tuple-element.19) | copy-start | bytes 786436
  76.1 28.3 %copy-start.6 = (f32[512,512]{1,0:T(8,128)S(1)}, f32[512,512]{1,0:T(8,128)}, u32[]{:S(2)}) copy-start(f32[512,512]{1,0:T(8,128)} %get-tuple-element.10) | copy-start | bytes 3145732
  76.1 28.3 %copy-start.7 = (f32[512,512]{1,0:T(8,128)S(1)}, f32[512,512]{1,0:T(8,128)}, u32[]{:S(2)}) copy-start(f32[512,512]{1,0:T(8,128)} %get-tuple-element.17) | copy-start | bytes 3145732
  76.3 26.1 %collective-permute-start.4 = (f32[2,256,128]{2,0,1:T(2,128)S(1)}, f32[2,256,128]{2,0,1:T(2,128)S(1)}, u32[]{:S(2)}, u32[]{:S(2)}) collective-permute-start(f32[2,256,128]{2,0,1:T(2,128)S(1)} %get-tuple-element.13), channel_id=1, source_target_pairs={{0,1},{1,2},{2,3},{3,4},{4,5},{5,6},{6,7},{7,8},{8,9},{9,10},{10,1... | collective-permute-start | bytes 786440 | tf_op jit(solution)/shard_map/ppermute | solution.py:28
  98.3 4.8 %collective-permute-start.5 = (f32[2,256,128]{2,0,1:T(2,128)S(1)}, f32[2,256,128]{2,0,1:T(2,128)S(1)}, u32[]{:S(2)}, u32[]{:S(2)}) collective-permute-start(f32[2,256,128]{2,0,1:T(2,128)S(1)} %get-tuple-element.14), channel_id=1, source_target_pairs={{1,0},{2,1},{3,2},{4,3},{5,4},{6,5},{7,6},{8,7},{9,8},{10,9},{11,1... | collective-permute-start | bytes 786440 | tf_op jit(solution)/shard_map/ppermute | solution.py:28
  104.4 140.0 %copy-start.2 = (f32[512,512]{1,0:T(8,128)}, f32[512,512]{1,0:T(8,128)S(1)}, u32[]{:S(2)}) copy-start(f32[512,512]{1,0:T(8,128)S(1)} %fusion.47) | copy-start | bytes 3145732
Sparse Core Ops, SparseCore 0:
  106.8 135.6 all-reduce.2
where the time goes:
time: 255 us; the launch traced here: 254 us
  waiting for transfers between devices  90.8 us (36%)
  blocking collectives  46.7 us (18%)
  starting transfers between devices  45.6 us (18%)
  matrix products  36 us (14%)
  between operations  16 us (6%)
  local copies, waits for them, and re-layouts  11.9 us (5%)
  other arithmetic  6.99 us (3%)
    psum x1, waiting for transfers between devices, per_device(): lax.psum((loss_part, grad_in, grad_out), 'rows')  88.5 us
    psum x1, blocking collectives, per_device(): lax.psum((loss_part, grad_in, grad_out), 'rows')  46.7 us
    ppermute x2, starting transfers between devices, shifted(): lax.ppermute(value, axis, [(source, source + steps) for source in range(f...  23.5 us
    ppermute x2, starting transfers between devices, extended(): lax.ppermute(lax.slice_in_dim(block, block.shape[dim] - width, None, axis...  19.4 us
    dot_general x2, matrix products, propagate(): result = jnp.einsum('bkij,bkjw->biw', masked, picked, precision=HIGH)  15.6 us
    gather x2, local copies, waits for them, and re-layouts, propagate(): picked = nearby[relative]  7.89 us
    dot_general x1, matrix products, per_device(): pre_hidden = jnp.dot(spread_in, weight_in, precision=HIGH)  6.74 us
    dot_general x1, matrix products, transposed(): jnp.einsum('bkij,biw->bkjw', masked, grads.reshape(blocks_here, block_row...  5.22 us
  transfers between devices with their start and end apart: 7, of which 4 were waited for; matrix products, arithmetic and copies ran while one was open for 2% of the time, Pallas kernels for 0%

commit v1 on v0

v1 whole, which is shorter than its diff:
```python
import functools

import jax
import jax.numpy as jnp
from jax import lax
from jax.experimental import pallas as pl
from jax.experimental.pallas import tpu as pltpu
from jax.sharding import PartitionSpec as P

REACH = 2
F32 = jnp.float32
BF16 = jnp.bfloat16
MESH = pl.DeviceIdType.MESH
PARTS = 3
SMALLEST = 16


def split(value):
    high = value.astype(BF16)
    return high, (value - high.astype(F32)).astype(BF16)


def mm(a_high, a_low, b_high, b_low):
    def one(a, b):
        return jnp.dot(a, b, preferred_element_type=F32)

    return one(a_high, b_high) + (one(a_high, b_low) + one(a_low, b_high))


def chunks(total, size, body):
    def step(i, carry):
        body(pl.ds(pl.multiple_of(i * size, size), size))
        return carry

    lax.fori_loop(0, total // size, step, 0)


def plan(n, rows):
    bits = list(range(n.bit_length() - 1))
    parts = []
    for part in range(PARTS):
        near = bits[1:4]
        turn = part % max(1, len(near))
        order = bits[:1] + near[turn:] + near[:turn] + bits[4:]
        length, offset, steps = rows, 0, []
        for bit in order:
            halves = length > SMALLEST
            if halves:
                length //= 2
            steps.append((bit, length, offset, halves))
            offset += length
        parts.append(steps)
    return parts, offset


def kernel(
    n, steps, index_ref, counts_ref, features, adjacency, labels, weight_in, weight_out,
    logits_ref, loss_ref, hidden_grad_ref, grad_in_ref, grad_out_ref,
    far_features, band, band_high, band_low, turned_high, turned_low,
    near_high, near_low, win_high, win_low, wout_high, wout_low, back_high, back_low,
    spread_high, spread_low, spread_t_high, spread_t_low, spread, hidden, slope, hid_high, hid_low, hid_t_high, hid_t_low,
    near_z, z_high, z_low, grad_high, grad_low, out_low, out_high, in_low, in_high, returned,
    acc, landing, full, loss_acc, loss_in,
    halo_send, halo_recv, part_send, part_recv, loss_send, loss_recv,
):
    me = lax.axis_index("rows")
    own = features.shape[0]
    block = adjacency.shape[2]
    here, slots = adjacency.shape[0], adjacency.shape[1]
    wide = 2 * REACH + 1
    hid = weight_in.shape[1]
    classes = weight_out.shape[1]
    has_low, has_high = me > 0, me < n - 1
    lower, upper = jnp.maximum(me - 1, 0), jnp.minimum(me + 1, n - 1)
    bits = n.bit_length() - 1

    barrier = pltpu.get_barrier_semaphore()
    for bit in range(bits):
        other = me + (1 << bit) - 2 * (1 << bit) * lax.rem(lax.div(me, 1 << bit), 2)
        pl.semaphore_signal(barrier, inc=1, device_id=(other,), device_id_type=MESH)

    @pl.when(has_low)
    def _():
        pl.semaphore_signal(barrier, inc=1, device_id=(lower,), device_id_type=MESH)

    @pl.when(has_high)
    def _():
        pl.semaphore_signal(barrier, inc=1, device_id=(upper,), device_id_type=MESH)

    pl.semaphore_wait(barrier, bits + jnp.where(has_low, 1, 0) + jnp.where(has_high, 1, 0))

    def exchange(slot, to_upper, at_upper, to_lower, at_lower):
        up = pltpu.make_async_remote_copy(
            src_ref=to_upper, dst_ref=at_upper, send_sem=halo_send.at[slot, 0], recv_sem=halo_recv.at[slot, 0],
            device_id=(upper,), device_id_type=MESH)
        down = pltpu.make_async_remote_copy(
            src_ref=to_lower, dst_ref=at_lower, send_sem=halo_send.at[slot, 1], recv_sem=halo_recv.at[slot, 1],
            device_id=(lower,), device_id_type=MESH)

        def start_up():
            @pl.when(has_high)
            def _():
                up.start()

        def start_down():
            @pl.when(has_low)
            def _():
                down.start()

        def finish():
            @pl.when(has_high)
            def _():
                up.wait_send()
                down.wait_recv()

            @pl.when(has_low)
            def _():
                down.wait_send()
                up.wait_recv()

            @pl.when(jnp.logical_not(has_low))
            def _():
                at_upper[...] = jnp.zeros(at_upper.shape, F32)

            @pl.when(jnp.logical_not(has_high))
            def _():
                at_lower[...] = jnp.zeros(at_lower.shape, F32)

        return start_up, start_down, finish

    start_up, start_down, finish_features = exchange(
        0, features, far_features.at[0], features, far_features.at[1])
    start_up()
    start_down()

    for b in range(here):
        weights = []
        for k in range(slots):
            relative = index_ref[b, k] - (me * here - REACH) - b
            used = k < counts_ref[b]
            weights.append([
                jnp.where(jnp.logical_and(used, relative == j), 1.0, 0.0).astype(F32) for j in range(wide)])

        def densify(rows, b=b, weights=weights):
            sums = [None] * wide
            for k in range(slots):
                tile = adjacency[b, k, rows, :]
                for j in range(wide):
                    term = weights[k][j] * tile
                    sums[j] = term if k == 0 else sums[j] + term
            for j in range(wide):
                columns = slice(j * block, (j + 1) * block)
                high, low = split(sums[j])
                band[b, rows, columns] = sums[j]
                band_high[b, rows, columns] = high
                band_low[b, rows, columns] = low

        chunks(block, 32, densify)
        for j in range(wide):
            columns = slice(j * block, (j + 1) * block)
            high, low = split(band[b, :, columns].T)
            turned_high[b, columns, :] = high
            turned_low[b, columns, :] = low
    win_high[...], win_low[...] = split(weight_in[...])
    wout_high[...], wout_low[...] = split(weight_out[...])
    back_high[...], back_low[...] = split(weight_out[...].T)
    middle = slice(own, 2 * own)
    near_high[middle, :], near_low[middle, :] = split(features[...])
    finish_features()
    for side, start in ((0, 0), (1, 2 * own)):
        rows = slice(start, start + own)
        near_high[rows, :], near_low[rows, :] = split(far_features[side])

    for b in range(here):
        rows = slice(b * block, (b + 1) * block)
        cols = slice(b * block, (b + wide) * block)
        value = mm(band_high[b], band_low[b], near_high[cols, :], near_low[cols, :])
        spread[rows, :] = value
        spread_high[rows, :], spread_low[rows, :] = split(value)

    slope[...] = mm(spread_high[...], spread_low[...], win_high[...], win_low[...])

    def gelu(rows):
        x = slope[rows, :]
        below = 0.5 * (1.0 + lax.erf(x * 0.7071067811865476))
        value = x * below
        hidden[rows, :] = value
        hid_high[rows, :], hid_low[rows, :] = split(value)
        slope[rows, :] = below + x * (jnp.exp(-0.5 * x * x) * 0.3989422804014327)

    chunks(own, 32, gelu)
    near_z[middle, :] = mm(hid_high[...], hid_low[...], wout_high[...], wout_low[...])

    start_up, start_down, finish_z = exchange(
        1, near_z.at[pl.ds(own, own)], near_z.at[pl.ds(0, own)],
        near_z.at[pl.ds(own, own)], near_z.at[pl.ds(2 * own, own)])
    start_up()
    start_down()
    for b in range(here):
        rows = slice(b * block, (b + 1) * block)
        spread_t_high[:, rows], spread_t_low[:, rows] = split(spread[rows, :].T)
        for c in range(hid // block):
            columns = slice(c * block, (c + 1) * block)
            hid_t_high[columns, rows], hid_t_low[columns, rows] = split(hidden[rows, columns].T)
    finish_z()
    z_high[...], z_low[...] = split(near_z[...])

    loss_acc[...] = jnp.zeros(loss_acc.shape, F32)
    for b in range(here):
        rows = slice(b * block, (b + 1) * block)
        cols = slice(b * block, (b + wide) * block)
        logits = mm(band_high[b], band_low[b], z_high[cols, :], z_low[cols, :])
        logits_ref[rows, :] = logits
        totals = jnp.log(jnp.sum(jnp.exp(logits), axis=1, keepdims=True))
        lanes = lax.broadcasted_iota(jnp.int32, logits.shape, 1)
        onehot = jnp.where(labels[rows, :] == lanes, 1.0, 0.0).astype(F32)
        row_loss = totals - jnp.sum(onehot * logits, axis=1, keepdims=True)
        loss_acc[...] += jnp.broadcast_to(jnp.sum(row_loss, axis=0, keepdims=True), loss_acc.shape)
        grad_high[rows, :], grad_low[rows, :] = split(jnp.exp(logits - totals) - onehot)

    def bucket(start):
        pieces = []
        for j in range(start // block, (start + own) // block):
            total = None
            for b in range(here):
                if 0 <= j - b < wide:
                    columns = slice((j - b) * block, (j - b + 1) * block)
                    rows = slice(b * block, (b + 1) * block)
                    term = mm(turned_high[b, columns, :], turned_low[b, columns, :], grad_high[rows, :], grad_low[rows, :])
                    total = term if total is None else total + term
            pieces.append(total)
        return pieces

    start_up, start_down, finish_returned = exchange(2, out_high, in_low, out_low, in_high)
    for i, piece in enumerate(bucket(2 * own)):
        out_high[i * block : (i + 1) * block, :] = piece
    start_up()
    for i, piece in enumerate(bucket(0)):
        out_low[i * block : (i + 1) * block, :] = piece
    start_down()
    for i, piece in enumerate(bucket(own)):
        returned[i * block : (i + 1) * block, :] = piece
    finish_returned()
    returned[...] = returned[...] + (in_low[...] + in_high[...])
    grad_high[...], grad_low[...] = split(returned[...])

    lows = [0] * PARTS

    def partner_of(bit):
        mine = lax.rem(lax.div(me, 1 << bit), 2)
        return mine, me + (1 << bit) - 2 * (1 << bit) * mine

    def start_step(part, s):
        bit, length, offset, halves = steps[part][s]
        mine, other = partner_of(bit)
        low = lows[part]
        source = low + (1 - mine) * length if halves else low
        copy = pltpu.make_async_remote_copy(
            src_ref=acc.at[part, pl.ds(pl.multiple_of(source, SMALLEST), length)],
            dst_ref=landing.at[part, pl.ds(offset, length)],
            send_sem=part_send.at[0, part, s], recv_sem=part_recv.at[0, part, s],
            device_id=(other,), device_id_type=MESH)
        copy.start()
        if halves:
            lows[part] = low + mine * length
        return copy

    def finish_step(part, s, copy):
        _, length, offset, _ = steps[part][s]
        copy.wait()
        rows = pl.ds(pl.multiple_of(lows[part], SMALLEST), length)
        acc[part, rows, :] = acc[part, rows, :] + landing[part, pl.ds(offset, length), :]

    def start_loss(s):
        _, other = partner_of(steps[0][s][0])
        copy = pltpu.make_async_remote_copy(
            src_ref=loss_acc, dst_ref=loss_in.at[s], send_sem=loss_send.at[s], recv_sem=loss_recv.at[s],
            device_id=(other,), device_id_type=MESH)
        copy.start()
        return copy

    acc[2] = mm(hid_t_high[...], hid_t_low[...], grad_high[...], grad_low[...])
    last_copy = start_step(2, 0)
    loss_copy = start_loss(0)
    hidden_grad_ref[...] = mm(grad_high[...], grad_low[...], back_high[...], back_low[...])

    def pre_grad(rows):
        hid_high[rows, :], hid_low[rows, :] = split(hidden_grad_ref[rows, :] * slope[rows, :])

    chunks(own, 32, pre_grad)
    first = []
    for part in range(2):
        columns = slice(part * hid // 2, (part + 1) * hid // 2)
        value = mm(spread_t_high[...], spread_t_low[...], hid_high[:, columns], hid_low[:, columns])
        for i in range(2):
            acc[part, i * block : (i + 1) * block, :] = value[:, i * classes : (i + 1) * classes]
        first.append(start_step(part, 0))
    copies = first + [last_copy]
    for s in range(bits):
        if s > 0:
            loss_copy = start_loss(s)
            copies = [start_step(part, s) for part in range(PARTS)]
        for part in range(PARTS):
            finish_step(part, s, copies[part])
        loss_copy.wait()
        loss_acc[...] = loss_acc[...] + loss_in[s]
    loss_ref[...] = loss_acc[...]

    for part in range(PARTS):
        rows = pl.ds(pl.multiple_of(lows[part], SMALLEST), steps[part][-1][1])
        full[part, rows, :] = acc[part, rows, :]
    for s in reversed(range(bits)):
        copies = []
        for part in range(PARTS):
            bit, length, _, halves = steps[part][s]
            if not halves:
                continue
            mine, other = partner_of(bit)
            rows = pl.ds(pl.multiple_of(lows[part], SMALLEST), length)
            copy = pltpu.make_async_remote_copy(
                src_ref=full.at[part, rows], dst_ref=full.at[part, rows],
                send_sem=part_send.at[1, part, s], recv_sem=part_recv.at[1, part, s],
                device_id=(other,), device_id_type=MESH)
            copy.start()
            copies.append(copy)
            lows[part] = lows[part] - mine * length
        for copy in copies:
            copy.wait()
    for part in range(2):
        for i in range(2):
            columns = slice((2 * part + i) * classes, (2 * part + i + 1) * classes)
            grad_in_ref[:, columns] = full[part, i * block : (i + 1) * block, :]
    grad_out_ref[...] = full[2]


def per_device(n, features, adjacency, block_index, block_counts, labels, weight_in, weight_out):
    own, f_in = features.shape
    here, _, block, _ = adjacency.shape
    hid, classes = weight_out.shape
    wide = 2 * REACH + 1
    rows = hid
    steps, landing = plan(n, rows)
    bits = n.bit_length() - 1

    def both(*shape):
        return [pltpu.VMEM(shape, BF16)] * 2

    def plain(*shape):
        return pltpu.VMEM(shape, F32)

    scratch = [
        plain(2, own, f_in), plain(here, block, wide * block), *both(here, block, wide * block),
        *both(here, wide * block, block), *both(3 * own, f_in), *both(f_in, hid), *both(hid, classes),
        *both(classes, hid), *both(own, f_in), *both(f_in, own), plain(own, f_in), plain(own, hid), plain(own, hid),
        *both(own, hid), *both(hid, own), plain(3 * own, classes), *both(3 * own, classes), *both(own, classes),
        plain(own, classes), plain(own, classes), plain(own, classes), plain(own, classes), plain(own, classes),
        plain(PARTS, rows, classes), plain(PARTS, landing, classes), plain(PARTS, rows, classes),
        plain(8, 128), plain(bits, 8, 128),
        pltpu.SemaphoreType.DMA((3, 2)), pltpu.SemaphoreType.DMA((3, 2)),
        pltpu.SemaphoreType.DMA((2, PARTS, bits)), pltpu.SemaphoreType.DMA((2, PARTS, bits)),
        pltpu.SemaphoreType.DMA((bits,)), pltpu.SemaphoreType.DMA((bits,)),
    ]
    shapes = [(own, classes), (8, 128), (own, hid), (f_in, hid), (hid, classes)]
    logits, loss, hidden_grad, grad_in, grad_out = pl.pallas_call(
        functools.partial(kernel, n, steps),
        out_shape=[jax.ShapeDtypeStruct(shape, F32) for shape in shapes],
        in_specs=[pl.BlockSpec(memory_space=pltpu.SMEM)] * 2 + [pl.BlockSpec(memory_space=pltpu.VMEM)] * 5,
        out_specs=[pl.BlockSpec(memory_space=pltpu.VMEM)] * 5,
        scratch_shapes=scratch,
        compiler_params=pltpu.CompilerParams(
            collective_id=0, has_side_effects=True, vmem_limit_bytes=56 * 1024 * 1024),
        name="step",
    )(block_index, block_counts, features, adjacency, labels[:, None], weight_in, weight_out)
    return (logits, loss[0, 0] / (own * n), hidden_grad, grad_in, grad_out)


def solution(mesh):
    in_specs = (
        P("rows", None),
        P("rows", None, None, None),
        P("rows", None),
        P("rows"),
        P("rows"),
        P(),
        P(),
    )
    out_specs = (P("rows", None), P(), P("rows", None), P(), P())
    return jax.shard_map(
        functools.partial(per_device, mesh.shape["rows"]),
        mesh=mesh, in_specs=in_specs, out_specs=out_specs, check_vma=False,
    )
```

time: 255 us -> 86 us (0.34)
  waiting for transfers between devices: 90.8 us -> 0 us
  Pallas kernels: 0 us -> 74 us
  blocking collectives: 46.7 us -> 0 us
  starting transfers between devices: 45.6 us -> 0 us
  matrix products: 36 us -> 0 us
  between operations: 16 us -> 2.43 us
  other arithmetic: 6.99 us -> 0 us
  local copies, waits for them, and re-layouts: 11.9 us -> 9.28 us
    psum x1 -> x0, waiting for transfers between devices: 88.5 us -> none  [per_device(): lax.psum((loss_part, grad_in, grad_out), 'rows')]
    pallas_call x0 -> x1, Pallas kernels: none -> 74 us  [per_device(): pl.pallas_call(functools.partial(kernel, n, steps), out_shape=[jax.ShapeD...]
    psum x1 -> x0, blocking collectives: 46.7 us -> none  [per_device(): lax.psum((loss_part, grad_in, grad_out), 'rows')]
    ppermute x6 -> x0, starting transfers between devices: 45.6 us -> none  [the longest x2 23.5 us: shifted(): lax.ppermute(value, axis, [(source, source + steps) for source in range(f...]
    dot_general x9 -> x0, matrix products: 36 us -> none  [the longest x2 15.6 us: propagate(): result = jnp.einsum('bkij,bkjw->biw', masked, picked, precision=HIGH)]
    gather x2 -> x0, local copies, waits for them, and re-layouts: 7.89 us -> none  [propagate(): picked = nearby[relative]]
    concatenate x2 -> x0, other arithmetic: 4.52 us -> none  [extended(): block = jnp.concatenate([low, block, high], axis=dim)]
    unnamed x18 -> x6, local copies, waits for them, and re-layouts: 3.58 us -> 6.51 us
  transfers between devices with their start and end apart: 7 -> 0, of which waited for: 4 -> 0; matrix products, arithmetic and copies ran while one was open for 2% -> 0% of each run, Pallas kernels for 0% -> 0%
where the time goes in v1:
time: 86 us; the launch traced here: 85.7 us
  Pallas kernels  74 us (86%)
  local copies, waits for them, and re-layouts  9.28 us (11%)
  between operations  2.43 us (3%)
    pallas_call x1, Pallas kernels, per_device(): pl.pallas_call(functools.partial(kernel, n, steps), out_shape=[jax.ShapeD...  74 us
    unnamed x6, local copies, waits for them, and re-layouts  6.51 us

profile of v1, /device:TPU:0, one launch (start us, length us, event | category | flops | bytes accessed | tf_op | source)
XLA Modules:
  0.0 85.7 jit_solution(9668514126328295034)
XLA Ops:
  0.6 1.5 %copy.12.labels = s32[512,1]{1,0:T(8,128)} copy(s32[512,1]{0,1:T(1,128)} %bitcast.2) | data formatting | bytes 4096 | tf_op jit(solution)/shard_map/broadcast_in_dim | solution.py:373
  2.2 74.0 %step.1 = (f32[512,128]{1,0:T(8,128)}, f32[8,128]{1,0:T(8,128)}, f32[512,512]{1,0:T(8,128)}, f32[256,512]{1,0:T(8,128)}, f32[512,128]{1,0:T(8,128)}) custom-call(s32[2,6]{1,0:T(2,128)} %index_ref.1, s32[2]{0:T(128)} %counts_ref.1, f32[512,256]{1,0:T(8,128)} %features.1, f32[2,6,256,256]{3,2,1,0:T(8,128)} %adjacency.1, s32[512,1]{1,0:T(8,128)} %copy.12.labels, ...), custom_call_target="tpu_custom_call" | custom-call | tf_op jit(solution)/shard_map/step/pallas_call | solution.py:364
  76.2 0.0 copy-start
  76.2 1.2 %slice.3 = f32[1,1]{1,0:T(1,128)} slice(f32[8,128]{1,0:T(8,128)} %get-tuple-element.11), slice={[0:1], [0:1]} | slice | bytes 8 | tf_op jit(solution)/shard_map/slice | solution.py:374
  78.1 1.7 %copy.17 = f32[512,128]{1,0:T(8,128)} copy(f32[512,128]{1,0:T(8,128)} %get-tuple-element.20) | data formatting | bytes 524288
  79.7 2.3 %copy.18 = f32[512,512]{1,0:T(8,128)} copy(f32[512,512]{1,0:T(8,128)} %get-tuple-element.22) | data formatting | bytes 2097152
  82.0 1.9 %copy.19 = f32[256,512]{1,0:T(8,128)} copy(f32[256,512]{1,0:T(8,128)} %get-tuple-element.23) | data formatting | bytes 1048576
  83.9 0.0 copy-done
  83.9 0.7 copy.20
Async XLA Ops:
  76.2 7.7 %copy-start = (f32[512,128]{1,0:T(8,128)S(1)}, f32[512,128]{1,0:T(8,128)}, u32[]{:S(2)}) copy-start(f32[512,128]{1,0:T(8,128)} %get-tuple-element.24) | copy-start | bytes 786436

commit v2 on v0

v2 whole, which is shorter than its diff:
```python
import functools

import jax
import jax.numpy as jnp
from jax import lax
from jax.experimental import pallas as pl
from jax.experimental.pallas import tpu as pltpu
from jax.sharding import PartitionSpec as P

REACH = 2
F32 = jnp.float32
BF16 = jnp.bfloat16
MESH = pl.DeviceIdType.MESH
PARTS = 3
SMALLEST = 16


def split(value):
    high = value.astype(BF16)
    return high, (value - high.astype(F32)).astype(BF16)


def mm(a_high, a_low, b_high, b_low):
    def one(a, b):
        return jnp.dot(a, b, preferred_element_type=F32)

    return one(a_high, b_high) + (one(a_high, b_low) + one(a_low, b_high))


def chunks(total, size, body):
    def step(i, carry):
        body(pl.ds(pl.multiple_of(i * size, size), size))
        return carry

    lax.fori_loop(0, total // size, step, 0)


def plan(n, rows):
    bits = list(range(n.bit_length() - 1))
    cut = min(len(bits), (rows // SMALLEST).bit_length() - 1)
    parts = []
    for part in range(PARTS):
        near = bits[1:4]
        turn = part % max(1, len(near))
        order = bits[:1] + near[turn:] + near[:turn] + bits[4:]
        groups = [(bit,) for bit in order[: cut - 2]] + [tuple(order[cut - 2 : cut])] + [(bit,) for bit in order[cut:]]
        length, offset, message, steps = rows, 0, 0, []
        for number, group in enumerate(groups):
            members = 1 << len(group)
            cuts = number < cut - 1
            if cuts:
                length //= members
            steps.append((group, length, offset, message, cuts))
            offset += (members - 1) * length
            message += members - 1
        parts.append(steps)
    return parts, offset, message


def kernel(
    n, steps, index_ref, counts_ref, features, adjacency_hbm, labels, weight_in, weight_out,
    logits_out, loss_out, hidden_grad_out, packed_out,
    adjacency, far_features, band, band_high, band_low, turned_high, turned_low,
    near_high, near_low, win_high, win_low, wout_high, wout_low, back_high, back_low,
    spread_high, spread_low, spread_t_high, spread_t_low, spread, hidden, slope, hid_high, hid_low, hid_t_high, hid_t_low,
    onehot_ref, near_z, z_high, z_low, logits_ref, grad_high, grad_low, out_low, out_high, in_low, in_high, returned,
    ret_high, ret_low, hidden_grad, acc, landing, full, loss_acc, loss_in,
    halo_send, halo_recv, part_send, part_recv, loss_send, loss_recv, local_sem,
):
    me = lax.axis_index("rows")
    own = features.shape[0]
    here, slots, block = adjacency.shape[:3]
    wide = 2 * REACH + 1
    hid = weight_in.shape[1]
    classes = weight_out.shape[1]
    has_low, has_high = me > 0, me < n - 1
    lower, upper = jnp.maximum(me - 1, 0), jnp.minimum(me + 1, n - 1)

    fetch = pltpu.make_async_copy(adjacency_hbm, adjacency, local_sem.at[0])
    fetch.start()

    def bit_of(bit):
        return lax.rem(lax.div(me, 1 << bit), 2)

    def member(group, delta):
        other, theirs, mine = me, 0, 0
        for position, bit in enumerate(group):
            weight = 1 << (len(group) - 1 - position)
            value = bit_of(bit)
            mine = mine + value * weight
            if delta & weight:
                other = other + (1 - 2 * value) * (1 << bit)
                theirs = theirs + (1 - value) * weight
            else:
                theirs = theirs + value * weight
        return other, theirs, mine

    partners = sorted({
        sum(1 << bit for position, bit in enumerate(step[0]) if delta & (1 << (len(step[0]) - 1 - position)))
        for part in steps for step in part for delta in range(1, 1 << len(step[0]))})
    barrier = pltpu.get_barrier_semaphore()
    for mask in partners:
        other = me
        for bit in range(n.bit_length() - 1):
            if mask >> bit & 1:
                other = other + (1 - 2 * bit_of(bit)) * (1 << bit)
        pl.semaphore_signal(barrier, inc=1, device_id=(other,), device_id_type=MESH)

    @pl.when(has_low)
    def _():
        pl.semaphore_signal(barrier, inc=1, device_id=(lower,), device_id_type=MESH)

    @pl.when(has_high)
    def _():
        pl.semaphore_signal(barrier, inc=1, device_id=(upper,), device_id_type=MESH)

    pl.semaphore_wait(barrier, len(partners) + jnp.where(has_low, 1, 0) + jnp.where(has_high, 1, 0))

    def rows_of(b):
        return slice(b * block, (b + 1) * block)

    class Halo:
        def __init__(self, slot, to_upper, from_lower, to_lower, from_upper):
            def copy(way, i, source, target, device):
                return pltpu.make_async_remote_copy(
                    src_ref=source.at[pl.ds(i * block, block)], dst_ref=target.at[pl.ds(i * block, block)],
                    send_sem=halo_send.at[slot, way, i], recv_sem=halo_recv.at[slot, way, i],
                    device_id=(device,), device_id_type=MESH)

            self.ups = [copy(0, i, to_upper, from_lower, upper) for i in range(here)]
            self.downs = [copy(1, i, to_lower, from_upper, lower) for i in range(here)]
            self.from_lower, self.from_upper = from_lower, from_upper

        def clear(self):
            @pl.when(jnp.logical_not(has_low))
            def _():
                self.from_lower[...] = jnp.zeros(self.from_lower.shape, F32)

            @pl.when(jnp.logical_not(has_high))
            def _():
                self.from_upper[...] = jnp.zeros(self.from_upper.shape, F32)

        def up(self, i):
            @pl.when(has_high)
            def _():
                self.ups[i].start()

        def down(self, i):
            @pl.when(has_low)
            def _():
                self.downs[i].start()

        def wait_lower(self, i):
            @pl.when(has_low)
            def _():
                self.ups[i].wait_recv()

        def wait_upper(self, i):
            @pl.when(has_high)
            def _():
                self.downs[i].wait_recv()

        def sent(self):
            @pl.when(has_high)
            def _():
                for copy in self.ups:
                    copy.wait_send()

            @pl.when(has_low)
            def _():
                for copy in self.downs:
                    copy.wait_send()

    first = Halo(0, features, far_features.at[0], features, far_features.at[1])
    for i in range(here):
        first.up(here - 1 - i)
        first.down(i)
    first.clear()

    win_high[...], win_low[...] = split(weight_in[...])
    wout_high[...], wout_low[...] = split(weight_out[...])
    back_high[...], back_low[...] = split(weight_out[...].T)
    middle = slice(own, 2 * own)
    near_high[middle, :], near_low[middle, :] = split(features[...])
    for b in range(here):
        lanes = lax.broadcasted_iota(jnp.int32, (classes, block), 0)
        onehot_ref[rows_of(b), :] = jnp.where(labels[:, rows_of(b)] == lanes, 1.0, 0.0).astype(F32).T
    fetch.wait()
    for b in range(here):
        weights = []
        for k in range(slots):
            relative = index_ref[b, k] - (me * here - REACH) - b
            used = k < counts_ref[b]
            weights.append([
                jnp.where(jnp.logical_and(used, relative == j), 1.0, 0.0).astype(F32) for j in range(wide)])

        def densify(rows, b=b, weights=weights):
            sums = [None] * wide
            for k in range(slots):
                tile = adjacency[b, k, rows, :]
                for j in range(wide):
                    term = weights[k][j] * tile
                    sums[j] = term if k == 0 else sums[j] + term
            for j in range(wide):
                columns = rows_of(j)
                high, low = split(sums[j])
                band[b, rows, columns] = sums[j]
                band_high[b, rows, columns] = high
                band_low[b, rows, columns] = low

        chunks(block, 32, densify)

    def propagate(total, high, low, b, first_block, last_block, fresh=False):
        first_block, last_block = max(first_block, b), min(last_block, b + wide - 1)
        if first_block > last_block:
            return
        columns = slice((first_block - b) * block, (last_block - b + 1) * block)
        window = slice(first_block * block, (last_block + 1) * block)
        value = mm(band_high[b, :, columns], band_low[b, :, columns], high[window, :], low[window, :])
        total[rows_of(b), :] = value if fresh else total[rows_of(b), :] + value

    for b in range(here):
        propagate(spread, near_high, near_low, b, REACH, REACH + here - 1, fresh=True)
    for b in range(here):
        for j in range(wide):
            high, low = split(band[b, :, rows_of(j)].T)
            turned_high[b, rows_of(j), :] = high
            turned_low[b, rows_of(j), :] = low

    def arrive_features(side, i):
        if side == 0:
            first.wait_lower(i)
        else:
            first.wait_upper(i)
        place = i if side == 0 else REACH + here + i
        near_high[rows_of(place), :], near_low[rows_of(place), :] = split(far_features[side, rows_of(i), :])
        for b in range(here):
            propagate(spread, near_high, near_low, b, place, place)

    second = Halo(
        1, near_z.at[pl.ds(own, own)], near_z.at[pl.ds(0, own)],
        near_z.at[pl.ds(own, own)], near_z.at[pl.ds(2 * own, own)])

    def forward(b):
        rows = rows_of(b)
        spread_high[rows, :], spread_low[rows, :] = split(spread[rows, :])
        slope[rows, :] = mm(spread_high[rows, :], spread_low[rows, :], win_high[...], win_low[...])

        def gelu(i, carry):
            part = pl.ds(pl.multiple_of(b * block + i * 32, 32), 32)
            x = slope[part, :]
            below = 0.5 * (1.0 + lax.erf(x * 0.7071067811865476))
            value = x * below
            hidden[part, :] = value
            hid_high[part, :], hid_low[part, :] = split(value)
            slope[part, :] = below + x * (jnp.exp(-0.5 * x * x) * 0.3989422804014327)
            return carry

        lax.fori_loop(0, block // 32, gelu, 0)
        near_z[own + b * block : own + (b + 1) * block, :] = mm(
            hid_high[rows, :], hid_low[rows, :], wout_high[...], wout_low[...])
        second.up(b)
        second.down(b)

    arrive_features(0, 1)
    arrive_features(1, 0)
    arrive_features(0, 0)
    forward(0)
    arrive_features(1, 1)
    forward(1)
    second.clear()

    z_high[middle, :], z_low[middle, :] = split(near_z[middle, :])
    for b in range(here):
        propagate(logits_ref, z_high, z_low, b, REACH, REACH + here - 1, fresh=True)
    for b in range(here):
        rows = rows_of(b)
        spread_t_high[:, rows], spread_t_low[:, rows] = split(spread[rows, :].T)
        for c in range(hid // block):
            hid_t_high[rows_of(c), rows], hid_t_low[rows_of(c), rows] = split(hidden[rows, rows_of(c)].T)
    for i in range(here):
        second.wait_lower(i)
        second.wait_upper(i)
        for place in (i, REACH + here + i):
            z_high[rows_of(place), :], z_low[rows_of(place), :] = split(near_z[rows_of(place), :])
            for b in range(here):
                propagate(logits_ref, z_high, z_low, b, place, place)
    place_logits = pltpu.make_async_copy(logits_ref, logits_out, local_sem.at[0])
    place_logits.start()

    loss_acc[...] = jnp.zeros(loss_acc.shape, F32)
    third = Halo(2, out_high, in_low, out_low, in_high)

    def softmax(b):
        rows = rows_of(b)
        logits = logits_ref[rows, :]
        totals = jnp.log(jnp.sum(jnp.exp(logits), axis=1, keepdims=True))
        onehot = onehot_ref[rows, :]
        row_loss = totals - jnp.sum(onehot * logits, axis=1, keepdims=True)
        loss_acc[...] += jnp.broadcast_to(jnp.sum(row_loss, axis=0, keepdims=True), loss_acc.shape)
        grad_high[rows, :], grad_low[rows, :] = split(jnp.exp(logits - totals) - onehot)

    def bucket(place):
        total = None
        for b in range(here):
            if 0 <= place - b < wide:
                term = mm(
                    turned_high[b, rows_of(place - b), :], turned_low[b, rows_of(place - b), :],
                    grad_high[rows_of(b), :], grad_low[rows_of(b), :])
                total = term if total is None else total + term
        return total

    softmax(0)
    out_low[rows_of(0), :] = bucket(0)
    third.down(0)
    softmax(1)
    for i in range(here):
        out_high[rows_of(i), :] = bucket(REACH + here + i)
        third.up(i)
        if i > 0:
            out_low[rows_of(i), :] = bucket(i)
            third.down(i)
    third.clear()
    for i in range(here):
        returned[rows_of(i), :] = bucket(REACH + i)

    lows = [0] * PARTS
    stages = [
        [(0, s) for s in range(len(part))] + [(1, s) for s in reversed(range(len(part))) if part[s][4]] for part in steps]
    reached = [0] * PARTS
    flying = [None] * PARTS

    def start_stage(part):
        phase, s = stages[part][reached[part]]
        group, length, offset, message, cuts = steps[part][s]
        low, copies = lows[part], []
        if phase == 1 and (reached[part] == 0 or stages[part][reached[part] - 1][0] == 0):
            rows = pl.ds(pl.multiple_of(low, SMALLEST), length)
            full[part, rows, :] = acc[part, rows, :]
        for delta in range(1, 1 << len(group)):
            other, theirs, mine = member(group, delta)
            if phase == 0:
                start = low + theirs * length if cuts else low
                source = acc.at[part, pl.ds(pl.multiple_of(start, SMALLEST), length)]
                target = landing.at[part, pl.ds(offset + (delta - 1) * length, length)]
            else:
                source = target = full.at[part, pl.ds(pl.multiple_of(low, SMALLEST), length)]
            copy = pltpu.make_async_remote_copy(
                src_ref=source, dst_ref=target, send_sem=part_send.at[phase, part, message + delta - 1],
                recv_sem=part_recv.at[phase, part, message + delta - 1], device_id=(other,), device_id_type=MESH)
            copy.start()
            copies.append(copy)
        if cuts:
            lows[part] = low + mine * length if phase == 0 else low - mine * length
        flying[part] = copies

    def finish_stage(part):
        phase, s = stages[part][reached[part]]
        group, length, offset, _, _ = steps[part][s]
        for copy in flying[part]:
            copy.wait()
        if phase == 0:
            rows = pl.ds(pl.multiple_of(lows[part], SMALLEST), length)
            total = acc[part, rows, :]
            for i in range(len(flying[part])):
                total = total + landing[part, pl.ds(offset + i * length, length), :]
            acc[part, rows, :] = total
        reached[part] += 1

    loss_flying = []

    def start_loss(s):
        group, _, _, message, _ = steps[0][s]
        loss_flying.clear()
        for delta in range(1, 1 << len(group)):
            other, _, _ = member(group, delta)
            place = message + delta - 1
            copy = pltpu.make_async_remote_copy(
                src_ref=loss_acc, dst_ref=loss_in.at[place], send_sem=loss_send.at[place], recv_sem=loss_recv.at[place],
                device_id=(other,), device_id_type=MESH)
            copy.start()
            loss_flying.append(copy)

    def finish_loss(s):
        for copy in loss_flying:
            copy.wait()
        total = loss_acc[...]
        for i in range(len(loss_flying)):
            total = total + loss_in[steps[0][s][3] + i]
        loss_acc[...] = total

    start_loss(0)
    values = [None] * 2
    for b in range(here):
        rows = rows_of(b)
        third.wait_lower(b)
        third.wait_upper(b)
        ret_high[rows, :], ret_low[rows, :] = split(returned[rows, :] + (in_low[rows, :] + in_high[rows, :]))
        value = mm(hid_t_high[:, rows], hid_t_low[:, rows], ret_high[rows, :], ret_low[rows, :])
        acc[2] = value if b == 0 else acc[2] + value
        if b == here - 1:
            start_stage(2)
        hidden_grad[rows, :] = mm(ret_high[rows, :], ret_low[rows, :], back_high[...], back_low[...])

        def pre_grad(i, carry, b=b):
            part = pl.ds(pl.multiple_of(b * block + i * 32, 32), 32)
            hid_high[part, :], hid_low[part, :] = split(hidden_grad[part, :] * slope[part, :])
            return carry

        lax.fori_loop(0, block // 32, pre_grad, 0)
        if b == here - 1:
            place_hidden = pltpu.make_async_copy(hidden_grad, hidden_grad_out, local_sem.at[1])
            place_hidden.start()
            finish_stage(2)
            start_stage(2)
            finish_loss(0)
            start_loss(1)
        for part in range(2):
            columns = slice(part * hid // 2, (part + 1) * hid // 2)
            value = mm(spread_t_high[:, rows], spread_t_low[:, rows], hid_high[rows, columns], hid_low[rows, columns])
            for i in range(2):
                piece = value[:, i * classes : (i + 1) * classes]
                acc[part, rows_of(i), :] = piece if b == 0 else acc[part, rows_of(i), :] + piece
            if b == here - 1:
                start_stage(part)

    placing = []
    loss_step = 1
    while any(reached[part] < len(stages[part]) for part in range(PARTS)):
        for part in (2, 0, 1):
            if reached[part] == len(stages[part]):
                continue
            finish_stage(part)
            if reached[part] < len(stages[part]):
                start_stage(part)
            else:
                copy = pltpu.make_async_copy(full.at[part], packed_out.at[part], local_sem.at[2 + part])
                copy.start()
                placing.append(copy)
        if loss_step < len(steps[0]):
            finish_loss(loss_step)
            loss_step += 1
            if loss_step < len(steps[0]):
                start_loss(loss_step)
            else:
                loss_out[...] = loss_acc[...]
    for halo in (first, second, third):
        halo.sent()
    for copy in [place_logits, place_hidden] + placing:
        copy.wait()


def place(total, logits, loss, hidden_grad, packed, logits_out, loss_out, hidden_grad_out, grad_in_out, grad_out_out, sems):
    f_in, hid = grad_in_out.shape
    classes = logits.shape[1]
    loss_out[0, 0] = loss[0, 0] * (1.0 / total)
    quarter = hidden_grad.shape[0] // 4
    pairs = [(logits, logits_out), (packed.at[2], grad_out_out)]
    for i in range(4):
        rows = pl.ds(i * quarter, quarter)
        pairs.append((hidden_grad.at[rows], hidden_grad_out.at[rows]))
    for i in range(hid // classes):
        pairs.append((
            packed.at[i // 2, pl.ds(i % 2 * f_in, f_in)], grad_in_out.at[:, pl.ds(i * classes, classes)]))
    copies = [pltpu.make_async_copy(source, target, sems.at[i]) for i, (source, target) in enumerate(pairs)]
    for copy in copies:
        copy.start()
    for copy in copies:
        copy.wait()


def per_device(n, features, adjacency, block_index, block_counts, labels, weight_in, weight_out):
    own, f_in = features.shape
    here, _, block, _ = adjacency.shape
    hid, classes = weight_out.shape
    wide = 2 * REACH + 1
    rows = hid
    steps, landing, messages = plan(n, rows)

    def both(*shape):
        return [pltpu.VMEM(shape, BF16)] * 2

    def plain(*shape):
        return pltpu.VMEM(shape, F32)

    scratch = [
        plain(*adjacency.shape), plain(2, own, f_in), plain(here, block, wide * block), *both(here, block, wide * block),
        *both(here, wide * block, block), *both(3 * own, f_in), *both(f_in, hid), *both(hid, classes),
        *both(classes, hid), *both(own, f_in), *both(f_in, own), plain(own, f_in), plain(own, hid), plain(own, hid),
        *both(own, hid), *both(hid, own), plain(own, classes), plain(3 * own, classes), *both(3 * own, classes),
        plain(own, classes), *both(own, classes),
        plain(own, classes), plain(own, classes), plain(own, classes), plain(own, classes), plain(own, classes),
        *both(own, classes), plain(own, hid),
        plain(PARTS, rows, classes), plain(PARTS, landing, classes), plain(PARTS, rows, classes),
        plain(8, 128), plain(messages, 8, 128),
        pltpu.SemaphoreType.DMA((3, 2, here)), pltpu.SemaphoreType.DMA((3, 2, here)),
        pltpu.SemaphoreType.DMA((2, PARTS, messages)), pltpu.SemaphoreType.DMA((2, PARTS, messages)),
        pltpu.SemaphoreType.DMA((messages,)), pltpu.SemaphoreType.DMA((messages,)),
        pltpu.SemaphoreType.DMA((2 + PARTS,)),
    ]
    smem, vmem, hbm = (pl.BlockSpec(memory_space=space) for space in (pltpu.SMEM, pltpu.VMEM, pltpu.HBM))

    def arrays(*shapes):
        return [jax.ShapeDtypeStruct(shape, F32) for shape in shapes]

    logits, loss, hidden_grad, packed = pl.pallas_call(
        functools.partial(kernel, n, steps),
        out_shape=arrays((own, classes), (8, 128), (own, hid), (PARTS, rows, classes)),
        in_specs=[smem, smem, vmem, hbm, vmem, vmem, vmem],
        out_specs=[hbm, vmem, hbm, hbm],
        scratch_shapes=scratch,
        compiler_params=pltpu.CompilerParams(
            collective_id=0, has_side_effects=True, vmem_limit_bytes=56 * 1024 * 1024),
        name="step",
    )(block_index, block_counts, features, adjacency, labels[None, :], weight_in, weight_out)
    logits, loss, hidden_grad, grad_in, grad_out = pl.pallas_call(
        functools.partial(place, float(own * n)),
        out_shape=arrays((own, classes), (1, 1), (own, hid), (f_in, hid), (hid, classes)),
        in_specs=[hbm, smem, hbm, hbm],
        out_specs=[hbm, smem, hbm, hbm, hbm],
        scratch_shapes=[pltpu.SemaphoreType.DMA((6 + hid // classes,))],
        compiler_params=pltpu.CompilerParams(vmem_limit_bytes=63 * 1024 * 1024),
        name="place",
    )(logits, loss, hidden_grad, packed)
    return (logits, loss[0, 0], hidden_grad, grad_in, grad_out)


def solution(mesh):
    in_specs = (
        P("rows", None),
        P("rows", None, None, None),
        P("rows", None),
        P("rows"),
        P("rows"),
        P(),
        P(),
    )
    out_specs = (P("rows", None), P(), P("rows", None), P(), P())
    return jax.shard_map(
        functools.partial(per_device, mesh.shape["rows"]),
        mesh=mesh, in_specs=in_specs, out_specs=out_specs, check_vma=False,
    )
```

time: 255 us -> 131 us (0.51)
  Pallas kernels: 0 us -> 130 us
  waiting for transfers between devices: 90.8 us -> 0 us
  blocking collectives: 46.7 us -> 0 us
  starting transfers between devices: 45.6 us -> 0 us
  matrix products: 36 us -> 0 us
  between operations: 16 us -> 0.64 us
  local copies, waits for them, and re-layouts: 11.9 us -> 0 us
  other arithmetic: 6.99 us -> 0 us
    pallas_call x0 -> x2, Pallas kernels: none -> 130 us  [the longest x1 66 us: per_device(): pl.pallas_call(functools.partial(place, float(own * n)), out_shape=arrays...]
    psum x1 -> x0, waiting for transfers between devices: 88.5 us -> none  [per_device(): lax.psum((loss_part, grad_in, grad_out), 'rows')]
    psum x1 -> x0, blocking collectives: 46.7 us -> none  [per_device(): lax.psum((loss_part, grad_in, grad_out), 'rows')]
    ppermute x6 -> x0, starting transfers between devices: 45.6 us -> none  [the longest x2 23.5 us: shifted(): lax.ppermute(value, axis, [(source, source + steps) for source in range(f...]
    dot_general x9 -> x0, matrix products: 36 us -> none  [the longest x2 15.6 us: propagate(): result = jnp.einsum('bkij,bkjw->biw', masked, picked, precision=HIGH)]
    gather x2 -> x0, local copies, waits for them, and re-layouts: 7.89 us -> none  [propagate(): picked = nearby[relative]]
    concatenate x2 -> x0, other arithmetic: 4.52 us -> none  [extended(): block = jnp.concatenate([low, block, high], axis=dim)]
    unnamed x18 -> x0, local copies, waits for them, and re-layouts: 3.58 us -> none
  transfers between devices with their start and end apart: 7 -> 0, of which waited for: 4 -> 0; matrix products, arithmetic and copies ran while one was open for 2% -> 0% of each run, Pallas kernels for 0% -> 0%
where the time goes in v2:
time: 131 us
  Pallas kernels  130 us (99%)
    pallas_call x1, Pallas kernels, per_device(): pl.pallas_call(functools.partial(place, float(own * n)), out_shape=arrays...  66 us
    pallas_call x1, Pallas kernels, per_device(): pl.pallas_call(functools.partial(kernel, n, steps), out_shape=arrays((own...  64.1 us

profile of v2, /device:TPU:0, one launch (start us, length us, event | category | flops | bytes accessed | tf_op | source)
XLA Modules:
  0.0 130.8 jit_solution(11186447581877384837)
XLA Ops:
  0.6 64.1 %step.1 = (f32[512,128]{1,0:T(8,128)}, f32[8,128]{1,0:T(8,128)}, f32[512,512]{1,0:T(8,128)}, f32[3,512,128]{2,1,0:T(8,128)}) custom-call(s32[2,6]{1,0:T(2,128)} %index_ref.1, s32[2]{0:T(128)} %counts_ref.1, f32[512,256]{1,0:T(8,128)} %features.1, f32[2,6,256,256]{3,2,1,0:T(8,128)} %adjacency_hbm.1, s32[1,512]{1,0:T(1,128)} %bitcast.2, f32[256,512]{1,0:T(8,128)} %weight_in.1, ...), custom_call_target="tpu_custom_call" | custom-call | tf_op jit(solution)/shard_map/step/pallas_call | solution.py:506
  64.8 66.0 %place.1 = (f32[512,128]{1,0:T(8,128)}, f32[1,1]{1,0:T(1,128)}, f32[512,512]{1,0:T(8,128)}, f32[256,512]{1,0:T(8,128)}, f32[512,128]{1,0:T(8,128)}) custom-call(f32[512,128]{1,0:T(8,128)} %get-tuple-element.14.logits, f32[8,128]{1,0:T(8,128)} %get-tuple-element.15.loss, f32[512,512]{1,0:T(8,128)} %get-tuple-element.16.hidden_grad, ...), custom_call_target="tpu_custom_call" | custom-call | tf_op jit(solution)/shard_map/place/pallas_call | solution.py:516

commit v3 on v2

--- a/solution.py
+++ b/solution.py
@@ -13,6 +13,7 @@
 MESH = pl.DeviceIdType.MESH
 PARTS = 3
 SMALLEST = 16
+TOGETHER = 3
 
 
 def split(value):
@@ -25,6 +26,12 @@
         return jnp.dot(a, b, preferred_element_type=F32)
 
     return one(a_high, b_high) + (one(a_high, b_low) + one(a_low, b_high))
+
+
+def mm_beside(a_high, a_low, b_both):
+    width = b_both.shape[1] // 2
+    wide = jnp.dot(a_high, b_both, preferred_element_type=F32)
+    return wide[:, :width] + (wide[:, width:] + jnp.dot(a_low, b_both[:, :width], preferred_element_type=F32))
 
 
 def chunks(total, size, body):
@@ -43,11 +50,11 @@
         near = bits[1:4]
         turn = part % max(1, len(near))
         order = bits[:1] + near[turn:] + near[:turn] + bits[4:]
-        groups = [(bit,) for bit in order[: cut - 2]] + [tuple(order[cut - 2 : cut])] + [(bit,) for bit in order[cut:]]
+        groups = [(bit,) for bit in order[: cut - TOGETHER]] + [tuple(order[cut - TOGETHER : cut])] + [(bit,) for bit in order[cut:]]
         length, offset, message, steps = rows, 0, 0, []
         for number, group in enumerate(groups):
             members = 1 << len(group)
-            cuts = number < cut - 1
+            cuts = number < cut - TOGETHER + 1
             if cuts:
                 length //= members
             steps.append((group, length, offset, message, cuts))
@@ -61,10 +68,10 @@
     n, steps, index_ref, counts_ref, features, adjacency_hbm, labels, weight_in, weight_out,
     logits_out, loss_out, hidden_grad_out, packed_out,
     adjacency, far_features, band, band_high, band_low, turned_high, turned_low,
-    near_high, near_low, win_high, win_low, wout_high, wout_low, back_high, back_low,
+    near_high, near_low, win_high, win_low, wout_both, back_high, back_low,
     spread_high, spread_low, spread_t_high, spread_t_low, spread, hidden, slope, hid_high, hid_low, hid_t_high, hid_t_low,
-    onehot_ref, near_z, z_high, z_low, logits_ref, grad_high, grad_low, out_low, out_high, in_low, in_high, returned,
-    ret_high, ret_low, hidden_grad, acc, landing, full, loss_acc, loss_in,
+    onehot_ref, near_z, z_both, logits_ref, grad_both, out_low, out_high, in_low, in_high, returned,
+    ret_both, hidden_grad, acc, landing, full, loss_acc, loss_in,
     halo_send, halo_recv, part_send, part_recv, loss_send, loss_recv, local_sem,
 ):
     me = lax.axis_index("rows")
@@ -178,7 +185,7 @@
     first.clear()
 
     win_high[...], win_low[...] = split(weight_in[...])
-    wout_high[...], wout_low[...] = split(weight_out[...])
+    wout_both[:, :classes], wout_both[:, classes:] = split(weight_out[...])
     back_high[...], back_low[...] = split(weight_out[...].T)
     middle = slice(own, 2 * own)
     near_high[middle, :], near_low[middle, :] = split(features[...])
@@ -216,7 +223,10 @@
             return
         columns = slice((first_block - b) * block, (last_block - b + 1) * block)
         window = slice(first_block * block, (last_block + 1) * block)
-        value = mm(band_high[b, :, columns], band_low[b, :, columns], high[window, :], low[window, :])
+        if low is None:
+            value = mm_beside(band_high[b, :, columns], band_low[b, :, columns], high[window, :])
+        else:
+            value = mm(band_high[b, :, columns], band_low[b, :, columns], high[window, :], low[window, :])
         total[rows_of(b), :] = value if fresh else total[rows_of(b), :] + value
 
     for b in range(here):
@@ -257,8 +267,8 @@
             return carry
 
         lax.fori_loop(0, block // 32, gelu, 0)
-        near_z[own + b * block : own + (b + 1) * block, :] = mm(
-            hid_high[rows, :], hid_low[rows, :], wout_high[...], wout_low[...])
+        near_z[own + b * block : own + (b + 1) * block, :] = mm_beside(
+            hid_high[rows, :], hid_low[rows, :], wout_both[...])
         second.up(b)
         second.down(b)
 
@@ -270,9 +280,9 @@
     forward(1)
     second.clear()
 
-    z_high[middle, :], z_low[middle, :] = split(near_z[middle, :])
-    for b in range(here):
-        propagate(logits_ref, z_high, z_low, b, REACH, REACH + here - 1, fresh=True)
+    z_both[middle, :classes], z_both[middle, classes:] = split(near_z[middle, :])
+    for b in range(here):
+        propagate(logits_ref, z_both, None, b, REACH, REACH + here - 1, fresh=True)
     for b in range(here):
         rows = rows_of(b)
         spread_t_high[:, rows], spread_t_low[:, rows] = split(spread[rows, :].T)
@@ -282,9 +292,9 @@
         second.wait_lower(i)
         second.wait_upper(i)
         for place in (i, REACH + here + i):
-            z_high[rows_of(place), :], z_low[rows_of(place), :] = split(near_z[rows_of(place), :])
+            z_both[rows_of(place), :classes], z_both[rows_of(place), classes:] = split(near_z[rows_of(place), :])
             for b in range(here):
-                propagate(logits_ref, z_high, z_low, b, place, place)
+                propagate(logits_ref, z_both, None, b, place, place)
     place_logits = pltpu.make_async_copy(logits_ref, logits_out, local_sem.at[0])
     place_logits.start()
 
@@ -298,15 +308,15 @@
         onehot = onehot_ref[rows, :]
         row_loss = totals - jnp.sum(onehot * logits, axis=1, keepdims=True)
         loss_acc[...] += jnp.broadcast_to(jnp.sum(row_loss, axis=0, keepdims=True), loss_acc.shape)
-        grad_high[rows, :], grad_low[rows, :] = split(jnp.exp(logits - totals) - onehot)
+        grad_both[rows, :classes], grad_both[rows, classes:] = split(jnp.exp(logits - totals) - onehot)
 
     def bucket(place):
         total = None
         for b in range(here):
             if 0 <= place - b < wide:
-                term = mm(
+                term = mm_beside(
                     turned_high[b, rows_of(place - b), :], turned_low[b, rows_of(place - b), :],
-                    grad_high[rows_of(b), :], grad_low[rows_of(b), :])
+                    grad_both[rows_of(b), :])
                 total = term if total is None else total + term
         return total
 
@@ -395,12 +405,12 @@
         rows = rows_of(b)
         third.wait_lower(b)
         third.wait_upper(b)
-        ret_high[rows, :], ret_low[rows, :] = split(returned[rows, :] + (in_low[rows, :] + in_high[rows, :]))
-        value = mm(hid_t_high[:, rows], hid_t_low[:, rows], ret_high[rows, :], ret_low[rows, :])
+        ret_both[rows, :classes], ret_both[rows, classes:] = split(returned[rows, :] + (in_low[rows, :] + in_high[rows, :]))
+        value = mm_beside(hid_t_high[:, rows], hid_t_low[:, rows], ret_both[rows, :])
         acc[2] = value if b == 0 else acc[2] + value
         if b == here - 1:
             start_stage(2)
-        hidden_grad[rows, :] = mm(ret_high[rows, :], ret_low[rows, :], back_high[...], back_low[...])
+        hidden_grad[rows, :] = mm(ret_both[rows, :classes], ret_both[rows, classes:], back_high[...], back_low[...])
 
         def pre_grad(i, carry, b=b):
             part = pl.ds(pl.multiple_of(b * block + i * 32, 32), 32)
@@ -450,22 +460,31 @@
         copy.wait()
 
 
-def place(total, logits, loss, hidden_grad, packed, logits_out, loss_out, hidden_grad_out, grad_in_out, grad_out_out, sems):
+def place(
+    total, logits, loss, hidden_grad, packed, logits_out, loss_out, hidden_grad_out, grad_in_out, grad_out_out,
+    logits_here, hidden_here, packed_here, sems,
+):
     f_in, hid = grad_in_out.shape
     classes = logits.shape[1]
-    loss_out[0, 0] = loss[0, 0] * (1.0 / total)
     quarter = hidden_grad.shape[0] // 4
-    pairs = [(logits, logits_out), (packed.at[2], grad_out_out)]
+    moves = []
     for i in range(4):
         rows = pl.ds(i * quarter, quarter)
-        pairs.append((hidden_grad.at[rows], hidden_grad_out.at[rows]))
+        moves.append((hidden_grad.at[rows], hidden_here.at[rows], hidden_grad_out.at[rows]))
     for i in range(hid // classes):
-        pairs.append((
-            packed.at[i // 2, pl.ds(i % 2 * f_in, f_in)], grad_in_out.at[:, pl.ds(i * classes, classes)]))
-    copies = [pltpu.make_async_copy(source, target, sems.at[i]) for i, (source, target) in enumerate(pairs)]
-    for copy in copies:
+        piece = (i // 2, pl.ds(i % 2 * f_in, f_in))
+        moves.append((packed.at[piece], packed_here.at[piece], grad_in_out.at[:, pl.ds(i * classes, classes)]))
+    moves.append((packed.at[2], packed_here.at[2], grad_out_out))
+    moves.append((logits, logits_here, logits_out))
+    fetches = [pltpu.make_async_copy(source, via, sems.at[0, i]) for i, (source, via, _) in enumerate(moves)]
+    stores = [pltpu.make_async_copy(via, target, sems.at[1, i]) for i, (_, via, target) in enumerate(moves)]
+    for copy in fetches:
         copy.start()
-    for copy in copies:
+    loss_out[0, 0] = loss[0, 0] * (1.0 / total)
+    for fetch, store in zip(fetches, stores):
+        fetch.wait()
+        store.start()
+    for copy in stores:
         copy.wait()
 
 
@@ -480,17 +499,20 @@
     def both(*shape):
         return [pltpu.VMEM(shape, BF16)] * 2
 
+    def beside(length):
+        return pltpu.VMEM((length, 2 * classes), BF16)
+
     def plain(*shape):
         return pltpu.VMEM(shape, F32)
 
     scratch = [
         plain(*adjacency.shape), plain(2, own, f_in), plain(here, block, wide * block), *both(here, block, wide * block),
-        *both(here, wide * block, block), *both(3 * own, f_in), *both(f_in, hid), *both(hid, classes),
+        *both(here, wide * block, block), *both(3 * own, f_in), *both(f_in, hid), beside(hid),
         *both(classes, hid), *both(own, f_in), *both(f_in, own), plain(own, f_in), plain(own, hid), plain(own, hid),
-        *both(own, hid), *both(hid, own), plain(own, classes), plain(3 * own, classes), *both(3 * own, classes),
-        plain(own, classes), *both(own, classes),
+        *both(own, hid), *both(hid, own), plain(own, classes), plain(3 * own, classes), beside(3 * own),
+        plain(own, classes), beside(own),
         plain(own, classes), plain(own, classes), plain(own, classes), plain(own, classes), plain(own, classes),
-        *both(own, classes), plain(own, hid),
+        beside(own), plain(own, hid),
         plain(PARTS, rows, classes), plain(PARTS, landing, classes), plain(PARTS, rows, classes),
         plain(8, 128), plain(messages, 8, 128),
         pltpu.SemaphoreType.DMA((3, 2, here)), pltpu.SemaphoreType.DMA((3, 2, here)),
@@ -518,7 +540,9 @@
         out_shape=arrays((own, classes), (1, 1), (own, hid), (f_in, hid), (hid, classes)),
         in_specs=[hbm, smem, hbm, hbm],
         out_specs=[hbm, smem, hbm, hbm, hbm],
-        scratch_shapes=[pltpu.SemaphoreType.DMA((6 + hid // classes,))],
+        scratch_shapes=[
+            plain(own, classes), plain(own, hid), plain(PARTS, rows, classes),
+            pltpu.SemaphoreType.DMA((2, 6 + hid // classes))],
         compiler_params=pltpu.CompilerParams(vmem_limit_bytes=63 * 1024 * 1024),
         name="place",
     )(logits, loss, hidden_grad, packed)

time: 131 us -> 66.5 us (0.51)
  Pallas kernels: 130 us -> 65.7 us
    pallas_call x1, Pallas kernels: 66 us -> 3.67 us  [per_device(): pl.pallas_call(functools.partial(place, float(own * n)), out_shape=arrays...]
    pallas_call x1, Pallas kernels: 64.1 us -> 62 us  [per_device(): pl.pallas_call(functools.partial(kernel, n, steps), out_shape=arrays((own...]
where the time goes in v3:
time: 66.5 us; the launch traced here: 66.3 us
  Pallas kernels  65.7 us (99%)
    pallas_call x1, Pallas kernels, per_device(): pl.pallas_call(functools.partial(kernel, n, steps), out_shape=arrays((own...  62 us
    pallas_call x1, Pallas kernels, per_device(): pl.pallas_call(functools.partial(place, float(own * n)), out_shape=arrays...  3.67 us

profile of v3, /device:TPU:0, one launch (start us, length us, event | category | flops | bytes accessed | tf_op | source)
XLA Modules:
  0.0 66.3 jit_solution(8332651037112523745)
XLA Ops:
  0.6 62.0 %step.1 = (f32[512,128]{1,0:T(8,128)}, f32[8,128]{1,0:T(8,128)}, f32[512,512]{1,0:T(8,128)}, f32[3,512,128]{2,1,0:T(8,128)}) custom-call(s32[2,6]{1,0:T(2,128)} %index_ref.1, s32[2]{0:T(128)} %counts_ref.1, f32[512,256]{1,0:T(8,128)} %features.1, f32[2,6,256,256]{3,2,1,0:T(8,128)} %adjacency_hbm.1, s32[1,512]{1,0:T(1,128)} %bitcast.2, f32[256,512]{1,0:T(8,128)} %weight_in.1, ...), custom_call_target="tpu_custom_call" | custom-call | tf_op jit(solution)/shard_map/step/pallas_call | solution.py:528
  62.6 3.7 %place.1 = (f32[512,128]{1,0:T(8,128)}, f32[1,1]{1,0:T(1,128)}, f32[512,512]{1,0:T(8,128)}, f32[256,512]{1,0:T(8,128)}, f32[512,128]{1,0:T(8,128)}) custom-call(f32[512,128]{1,0:T(8,128)} %get-tuple-element.14.logits, f32[8,128]{1,0:T(8,128)} %get-tuple-element.15.loss, f32[512,512]{1,0:T(8,128)} %get-tuple-element.16.hidden_grad, ...), custom_call_target="tpu_custom_call" | custom-call | tf_op jit(solution)/shard_map/place/pallas_call | solution.py:538

commit v4 on v3

--- a/solution.py
+++ b/solution.py
@@ -231,11 +231,6 @@
 
     for b in range(here):
         propagate(spread, near_high, near_low, b, REACH, REACH + here - 1, fresh=True)
-    for b in range(here):
-        for j in range(wide):
-            high, low = split(band[b, :, rows_of(j)].T)
-            turned_high[b, rows_of(j), :] = high
-            turned_low[b, rows_of(j), :] = low
 
     def arrive_features(side, i):
         if side == 0:
@@ -288,6 +283,11 @@
         spread_t_high[:, rows], spread_t_low[:, rows] = split(spread[rows, :].T)
         for c in range(hid // block):
             hid_t_high[rows_of(c), rows], hid_t_low[rows_of(c), rows] = split(hidden[rows, rows_of(c)].T)
+    for b in range(here):
+        for j in range(wide):
+            high, low = split(band[b, :, rows_of(j)].T)
+            turned_high[b, rows_of(j), :] = high
+            turned_low[b, rows_of(j), :] = low
     for i in range(here):
         second.wait_lower(i)
         second.wait_upper(i)

time: 66.5 us -> 66.4 us (level)
  no operation moved by 1% of the time
where the time goes in v4:
time: 66.4 us; the launch traced here: 66.2 us
  Pallas kernels  65.5 us (99%)
    pallas_call x1, Pallas kernels, per_device(): pl.pallas_call(functools.partial(kernel, n, steps), out_shape=arrays((own...  61.9 us
    pallas_call x1, Pallas kernels, per_device(): pl.pallas_call(functools.partial(place, float(own * n)), out_shape=arrays...  3.67 us

profile of v4, /device:TPU:0, one launch (start us, length us, event | category | flops | bytes accessed | tf_op | source)
XLA Modules:
  0.0 66.2 jit_solution(712669068068210210)
XLA Ops:
  0.6 61.9 %step.1 = (f32[512,128]{1,0:T(8,128)}, f32[8,128]{1,0:T(8,128)}, f32[512,512]{1,0:T(8,128)}, f32[3,512,128]{2,1,0:T(8,128)}) custom-call(s32[2,6]{1,0:T(2,128)} %index_ref.1, s32[2]{0:T(128)} %counts_ref.1, f32[512,256]{1,0:T(8,128)} %features.1, f32[2,6,256,256]{3,2,1,0:T(8,128)} %adjacency_hbm.1, s32[1,512]{1,0:T(1,128)} %bitcast.2, f32[256,512]{1,0:T(8,128)} %weight_in.1, ...), custom_call_target="tpu_custom_call" | custom-call | tf_op jit(solution)/shard_map/step/pallas_call | solution.py:528
  62.5 3.7 %place.1 = (f32[512,128]{1,0:T(8,128)}, f32[1,1]{1,0:T(1,128)}, f32[512,512]{1,0:T(8,128)}, f32[256,512]{1,0:T(8,128)}, f32[512,128]{1,0:T(8,128)}) custom-call(f32[512,128]{1,0:T(8,128)} %get-tuple-element.14.logits, f32[8,128]{1,0:T(8,128)} %get-tuple-element.15.loss, f32[512,512]{1,0:T(8,128)} %get-tuple-element.16.hidden_grad, ...), custom_call_target="tpu_custom_call" | custom-call | tf_op jit(solution)/shard_map/place/pallas_call | solution.py:538
